TPU v7x, 256 devices: a whole 4x4x8 slice. The times are simulated.
256 devices in a mesh: group: 4 (over z_lo, core), tile: 64 (over x, z_hi, y).
Axes of the slice: x: 4, y: 4, z: 8 (z_hi: 4, z_lo: 2; z = z_hi * 2 + z_lo), core: 2. Of those that a mesh axis runs over, the one named last changes fastest.
Arguments:
- object_slices: bfloat16 [4, 2048, 8192], P(None, 'group', 'tile'), may hold values from -4 to 4
- probe: float32 [1024, 256], replicated, may hold values from -6 to 6
- mid_waves: bfloat16 [4, 64, 3, 2, 2, 256, 256], P('group', 'tile'), may hold values from -160 to 160
- amplitudes: bfloat16 [4, 64, 3, 256, 256], P('group', 'tile'), may hold values from 0.19921875 to 4
- row_offsets: int32 [4, 64, 3], P('group', 'tile'), may hold values from 0 to 256
- col_offsets: int32 [4, 64, 3], P('group', 'tile'), may hold values from 0 to 128
Outputs:
- object_new: float32 [4, 2048, 8192], P(None, 'group', 'tile')
- probe_new: float32 [1024, 256], P('tile')
All inputs are finite; a program needn't handle non-finite values.
Results may differ from a plain program's by a relative error of at most 0.0003.
Values may be sent and summed in bfloat16 or wider, within the bound.
A program may use at most 128 MiB of HBM per device.

v0:
```python
import jax
import jax.numpy as jnp
from jax import lax
from jax.sharding import PartitionSpec as P

phase_rate = 0.25
floor_level = 0.5
object_step = 0.5
probe_step = 0.5
epsilon = 1e-06


def with_halo(cells, sides, width):
    for axis, dim in sides:
        count = lax.axis_size(axis)
        ends = count - 1
        head = lax.slice_in_dim(cells, 0, width, axis=dim)
        tail = lax.slice_in_dim(cells, cells.shape[dim] - width, cells.shape[dim], axis=dim)
        cells = jnp.concatenate(
            [
                lax.ppermute(tail, axis, [(i, (i + 1) % count) for i in range(ends)]),
                cells,
                lax.ppermute(head, axis, [((i + 1) % count, i) for i in range(ends)]),
            ],
            axis=dim,
        )
    return cells


def passed_along(block, axis, distance):
    devices = range(lax.axis_size(axis))
    route = [(i - distance, i) for i in devices if i - distance in devices]
    return lax.ppermute(block, axis, route)


def dft_tables(length):
    index = jnp.arange(length, dtype=jnp.int32)
    product = index[:, None] * index[None, :] % length
    angle = product.astype(jnp.float32) * (2.0 * jnp.pi / length)
    norming = 1.0 / jnp.sqrt(jnp.float32(length))
    return (jnp.cos(angle) * norming, jnp.sin(angle) * norming)


def back_tables(length):
    freq = jnp.arange(length, dtype=jnp.int32)
    freq = jnp.where(freq < length // 2, freq, freq - length).astype(jnp.float32)
    phase = (
        2.0
        * jnp.pi
        * phase_rate
        / length
        * (freq[:, None] * freq[:, None] + freq[None, :] * freq[None, :])
    )
    return (jnp.cos(phase), jnp.sin(phase))


def spectral(real_part, imag_part, cos_table, sin_table, direction):
    highest = lax.Precision.HIGHEST
    signed = sin_table * direction
    left_real = jnp.matmul(cos_table, real_part, precision=highest) - jnp.matmul(
        signed, imag_part, precision=highest
    )
    left_imag = jnp.matmul(cos_table, imag_part, precision=highest) + jnp.matmul(
        signed, real_part, precision=highest
    )
    out_real = jnp.matmul(left_real, cos_table, precision=highest) - jnp.matmul(
        left_imag, signed, precision=highest
    )
    out_imag = jnp.matmul(left_imag, cos_table, precision=highest) + jnp.matmul(
        left_real, signed, precision=highest
    )
    return (out_real, out_imag)


def shards(object_slices, probe, mid_waves, amplitudes, row_offsets, col_offsets):
    row_count = object_slices.shape[1]
    strip_width = object_slices.shape[2]
    probe_size = probe.shape[1]
    mode_count = probe.shape[0] // (2 * probe_size)
    padded = with_halo(object_slices, (("tile", 2),), strip_width).astype(jnp.float32)
    probe_parts = probe.reshape(2, mode_count, probe_size, probe_size)
    cos_table, sin_table = dft_tables(probe_size)
    kernel_real, kernel_imag = back_tables(probe_size)
    grad_obj = jnp.zeros(padded.shape, jnp.float32)
    grad_probe = jnp.zeros((2, mode_count, probe_size, probe_size), jnp.float32)
    anchor = jnp.zeros((), jnp.int32)
    for position in range(mid_waves.shape[2]):
        row_at = row_offsets[0, 0, position]
        col_at = col_offsets[0, 0, position]
        patch = lax.dynamic_slice(padded, (anchor, row_at, col_at), (4, probe_size, probe_size))
        first_real, first_imag, second_real, second_imag = (patch[0], patch[1], patch[2], patch[3])
        wave = mid_waves[0, 0, position].astype(jnp.float32)
        mid_real, mid_imag = (wave[0], wave[1])
        amp = amplitudes[0, 0, position].astype(jnp.float32)
        exit_real = mid_real * second_real - mid_imag * second_imag
        exit_imag = mid_real * second_imag + mid_imag * second_real
        far_real, far_imag = spectral(exit_real, exit_imag, cos_table, sin_table, -1.0)
        power = jnp.sum(far_real * far_real + far_imag * far_imag, axis=0)
        factor = 1.0 - amp / jnp.maximum(jnp.sqrt(power), floor_level)
        chi_real, chi_imag = spectral(
            far_real * factor, far_imag * factor, cos_table, sin_table, 1.0
        )
        second_grad_real = jnp.sum(mid_real * chi_real + mid_imag * chi_imag, axis=0)
        second_grad_imag = jnp.sum(mid_real * chi_imag - mid_imag * chi_real, axis=0)
        back_real = second_real * chi_real + second_imag * chi_imag
        back_imag = second_real * chi_imag - second_imag * chi_real
        spec_real, spec_imag = spectral(back_real, back_imag, cos_table, sin_table, -1.0)
        turned_real = spec_real * kernel_real - spec_imag * kernel_imag
        turned_imag = spec_real * kernel_imag + spec_imag * kernel_real
        wave_real, wave_imag = spectral(turned_real, turned_imag, cos_table, sin_table, 1.0)
        first_grad_real = jnp.sum(probe_parts[0] * wave_real + probe_parts[1] * wave_imag, axis=0)
        first_grad_imag = jnp.sum(probe_parts[0] * wave_imag - probe_parts[1] * wave_real, axis=0)
        probe_real = first_real * wave_real + first_imag * wave_imag
        probe_imag = first_real * wave_imag - first_imag * wave_real
        grad_probe = grad_probe + jnp.stack([probe_real, probe_imag])
        update = jnp.stack([first_grad_real, first_grad_imag, second_grad_real, second_grad_imag])
        previous = lax.dynamic_slice(
            grad_obj, (anchor, row_at, col_at), (4, probe_size, probe_size)
        )
        grad_obj = lax.dynamic_update_slice(grad_obj, previous + update, (anchor, row_at, col_at))
    left_rim = grad_obj[:, :, :strip_width]
    right_rim = grad_obj[:, :, 2 * strip_width :]
    own_grad = grad_obj[:, :, strip_width : 2 * strip_width]
    own_grad = own_grad + passed_along(left_rim, "tile", -1)
    own_grad = own_grad + passed_along(right_rim, "tile", 1)
    object_squares = jnp.sum(own_grad * own_grad)
    flat_probe = grad_probe.reshape(2 * mode_count * probe_size, probe_size)
    share = flat_probe.shape[0] // lax.axis_size("tile")
    start_row = lax.axis_index("tile") * share
    probe_total = lax.psum(flat_probe, ("group", "tile"))
    probe_shard = lax.dynamic_slice_in_dim(probe_total, start_row, share, 0)
    object_total = lax.psum(object_squares, ("group", "tile"))
    probe_squares = jnp.sum(probe_total * probe_total)
    object_count = 4 * row_count * strip_width * lax.axis_size("group") * lax.axis_size("tile")
    object_rms = jnp.sqrt(object_total / object_count + epsilon)
    object_new = padded[:, :, strip_width : 2 * strip_width] - object_step * own_grad / object_rms
    probe_count = 2 * mode_count * probe_size * probe_size
    probe_rms = jnp.sqrt(probe_squares / probe_count + epsilon)
    probe_rows = lax.dynamic_slice_in_dim(probe, start_row, share, 0)
    probe_new = probe_rows - probe_step * probe_shard / probe_rms
    return (object_new, probe_new)


def solution(mesh):
    return jax.shard_map(
        shards,
        mesh=mesh,
        in_specs=(
            P(None, "group", "tile"),
            P(),
            P("group", "tile", None, None, None, None, None),
            P("group", "tile", None, None, None),
            P("group", "tile", None),
            P("group", "tile", None),
        ),
        out_specs=(P(None, "group", "tile"), P("tile", None)),
        check_vma=False,
    )
```

profile of v0, /device:TPU:1, one launch (start us, length us, event | category | flops | bytes accessed | tf_op | source)
XLA Modules:
  0.0 642.6 jit_solution(9129326133849237512)
XLA Ops:
  7.2 5.0 collective-permute-start
  41.3 2.0 fusion.156
  66.3 1.8 convolution_subtract_fusion.14
  78.2 2.1 fusion.13
  85.0 2.4 add_reduce_fusion.3
  90.7 1.9 fusion.11
  104.0 1.9 fusion.42
  115.6 2.1 add_reduce_fusion.6
  141.0 1.8 fusion.117
  145.9 2.4 add_reduce_fusion
  153.4 2.0 fusion.110
  190.0 1.8 convolution_subtract_fusion
  193.4 5.2 add_bitcast_fusion
  199.8 16.8 %dynamic_update_slice.9 = f32[4,512,384]{2,1,0:T(8,128)S(1)} dynamic-update-slice(f32[4,512,384]{2,1,0:T(8,128)S(1)} %broadcast_in_dim.2, f32[4,256,256]{2,1,0:T(8,128)} %pad_maximum_fusion, s32[]{:T(128)} %constant.21.clone.1, s32[]{:T(128)S(6)} %select_n.264, s32[]{:T(128)S(6)} %select_n.265) | dynamic-update-slice | bytes 2097156 | tf_op jit(solution)/shard_map/dynamic_update_slice | solution.py:120
  216.6 2.5 maximum_add_fusion
  219.1 15.5 %dynamic_update_slice.10 = f32[4,512,384]{2,1,0:T(8,128)S(1)} dynamic-update-slice(f32[4,512,384]{2,1,0:T(8,128)S(1)} %dynamic_update_slice.9, f32[4,256,256]{2,1,0:T(8,128)} %maximum_add_fusion, s32[]{:T(128)} %constant.21.clone.1, s32[]{:T(128)S(6)} %select_n.267, s32[]{:T(128)S(6)} %select_n.268) | dynamic-update-slice | bytes 2097156 | tf_op jit(solution)/shard_map/dynamic_update_slice | solution.py:120
  234.6 2.5 maximum_add_fusion.1
  237.1 15.6 %dynamic_update_slice.11 = f32[4,512,384]{2,1,0:T(8,128)S(1)} dynamic-update-slice(f32[4,512,384]{2,1,0:T(8,128)S(1)} %dynamic_update_slice.10, f32[4,256,256]{2,1,0:T(8,128)} %maximum_add_fusion.1, s32[]{:T(128)} %constant.21.clone.1, s32[]{:T(128)S(6)} %select_n.269, s32[]{:T(128)S(6)} %select_n.270) | dynamic-update-slice | bytes 2097156 | tf_op jit(solution)/shard_map/dynamic_update_slice | solution.py:120
  255.7 5.0 collective-permute-start.3
  261.9 285.6 %all-reduce.2.cloned.1.call-done = f32[1024,256]{1,0:T(8,128)} async-done(((f32[1024,256]{1,0:T(8,128)}), f32[1024,256]{1,0:T(8,128)}) %all-reduce.2.cloned.1.call-update) | async-done | bytes 1048592 | tf_op jit(solution)/shard_map/psum | solution.py:130
  547.5 2.1 multiply_reduce_fusion
  550.3 2.4 multiply_reduce_fusion.1
  554.1 77.5 %psum.14 = f32[]{:T(128)} all-reduce(f32[]{:T(128)} %multiply_reduce_fusion.1), channel_id=1, replica_groups=mesh['group'=4,'tile'=64] {'group','tile'}, use_global_device_ids=true, to_apply=%region_16.17 | all-reduce | flops 1 | bytes 8 | tf_op jit(solution)/shard_map/psum | solution.py:132
  632.3 3.0 slice_subtract_fusion
  (126 shorter events, 153.6 us)
Async XLA Ops:
  7.2 23.0 %copy-start.7 = (bf16[1,1,3,2,2,256,256]{6,5,4,3,2,1,0:T(8,128)(2,1)S(1)}, bf16[1,1,3,2,2,256,256]{6,5,4,3,2,1,0:T(8,128)(2,1)}, u32[]{:S(2)}) copy-start(bf16[1,1,3,2,2,256,256]{6,5,4,3,2,1,0:T(8,128)(2,1)} %param.8) | copy-start | bytes 4718596
  7.2 540.3 %all-reduce.2.cloned.1.call-start = ((), (), s32[]{:S(2)}) async-start(), calls=%async_computation | async-start | bytes 2097152 | tf_op jit(solution)/shard_map/psum | solution.py:130
  7.2 23.2 %collective-permute-start = (bf16[4,512,128]{2,1,0:T(8,128)(2,1)}, bf16[4,512,128]{2,1,0:T(8,128)(2,1)}, u32[]{:S(2)}, u32[]{:S(2)}) collective-permute-start(bf16[4,512,128]{2,1,0:T(8,128)(2,1)} %param.6), channel_id=1, source_target_pairs={{0,1},{1,2},{2,3},{3,4},{4,5},{5,6},{6,7},{7,8},{8,9},{9,10},{10,1... | collective-permute-start | bytes 1572872 | tf_op jit(solution)/shard_map/ppermute | solution.py:21
  12.2 18.3 %collective-permute-start.1 = (bf16[4,512,128]{2,1,0:T(8,128)(2,1)}, bf16[4,512,128]{2,1,0:T(8,128)(2,1)}, u32[]{:S(2)}, u32[]{:S(2)}) collective-permute-start(bf16[4,512,128]{2,1,0:T(8,128)(2,1)} %param.6), channel_id=1, source_target_pairs={{1,0},{2,1},{3,2},{4,3},{5,4},{6,5},{7,6},{8,7},{9,8},{10,9},{11,1... | collective-permute-start | bytes 1572872 | tf_op jit(solution)/shard_map/ppermute | solution.py:23
  25.3 5.2 copy-start.8
  31.9 13.2 %copy-start = (f32[4,512,384]{2,1,0:T(8,128)}, f32[4,512,384]{2,1,0:T(8,128)S(1)}, u32[]{:S(2)}) copy-start(f32[4,512,384]{2,1,0:T(8,128)S(1)} %maximum_convert_fusion) | copy-start | bytes 9437188
  68.1 4.8 copy-start.9
  252.7 8.0 %copy-start.1 = (f32[1,2,256,256]{3,2,1,0:T(8,128)S(1)}, f32[1,2,256,256]{3,2,1,0:T(8,128)}, u32[]{:S(2)}) copy-start(f32[1,2,256,256]{3,2,1,0:T(8,128)} %get-tuple-element.32) | copy-start | bytes 1572868
  252.7 8.0 %copy-start.2 = (f32[1,2,256,256]{3,2,1,0:T(8,128)S(1)}, f32[1,2,256,256]{3,2,1,0:T(8,128)}, u32[]{:S(2)}) copy-start(f32[1,2,256,256]{3,2,1,0:T(8,128)} %get-tuple-element.33) | copy-start | bytes 1572868
  252.7 8.0 %copy-start.3 = (f32[1,2,256,256]{3,2,1,0:T(8,128)S(1)}, f32[1,2,256,256]{3,2,1,0:T(8,128)}, u32[]{:S(2)}) copy-start(f32[1,2,256,256]{3,2,1,0:T(8,128)} %get-tuple-element.47) | copy-start | bytes 1572868
  252.7 8.0 %copy-start.4 = (f32[1,2,256,256]{3,2,1,0:T(8,128)S(1)}, f32[1,2,256,256]{3,2,1,0:T(8,128)}, u32[]{:S(2)}) copy-start(f32[1,2,256,256]{3,2,1,0:T(8,128)} %get-tuple-element.48) | copy-start | bytes 1572868
  252.8 7.9 %copy-start.5 = (f32[1,2,256,256]{3,2,1,0:T(8,128)S(1)}, f32[1,2,256,256]{3,2,1,0:T(8,128)}, u32[]{:S(2)}) copy-start(f32[1,2,256,256]{3,2,1,0:T(8,128)} %get-tuple-element.49) | copy-start | bytes 1572868
  252.8 7.9 %copy-start.6 = (f32[1,2,256,256]{3,2,1,0:T(8,128)S(1)}, f32[1,2,256,256]{3,2,1,0:T(8,128)}, u32[]{:S(2)}) copy-start(f32[1,2,256,256]{3,2,1,0:T(8,128)} %get-tuple-element.50) | copy-start | bytes 1572868
  254.3 296.0 %collective-permute-start.2 = (f32[4,512,128]{2,1,0:T(8,128)}, f32[4,512,128]{2,1,0:T(8,128)}, u32[]{:S(2)}, u32[]{:S(2)}) collective-permute-start(f32[4,512,128]{2,1,0:T(8,128)} %get-tuple-element.30), channel_id=1, source_target_pairs={{1,0},{2,1},{3,2},{4,3},{5,4},{6,5},{7,6},{8,7},{9,8},{10,9},{11,1... | collective-permute-start | bytes 3145736 | tf_op jit(solution)/shard_map/ppermute | solution.py:33
  255.7 294.6 %collective-permute-start.3 = (f32[4,512,128]{2,1,0:T(8,128)}, f32[4,512,128]{2,1,0:T(8,128)}, u32[]{:S(2)}, u32[]{:S(2)}) collective-permute-start(f32[4,512,128]{2,1,0:T(8,128)} %get-tuple-element.31), channel_id=1, source_target_pairs={{0,1},{1,2},{2,3},{3,4},{4,5},{5,6},{6,7},{7,8},{8,9},{9,10},{10,1... | collective-permute-start | bytes 3145736 | tf_op jit(solution)/shard_map/ppermute | solution.py:33
Sparse Core Ops, SparseCore 0:
  262.0 285.3 all-reduce.1
where the time goes:
time: 653 us; the launch traced here: 643 us
  waiting for transfers between devices  286 us (44%)
  matrix products  165 us (25%)
  blocking collectives  77.5 us (12%)
  local copies, waits for them, and re-layouts  54.7 us (8%)
  between operations  28.3 us (4%)
  other arithmetic  19.1 us (3%)
  starting transfers between devices  12.7 us (2%)
    psum x1, waiting for transfers between devices, shards(): probe_total = lax.psum(flat_probe, ('group', 'tile'))  286 us
    psum x1, blocking collectives, shards(): object_total = lax.psum(object_squares, ('group', 'tile'))  77.5 us
    dynamic_update_slice x3, local copies, waits for them, and re-layouts, shards(): lax.dynamic_update_slice(grad_obj, previous + update, (anchor, row_at, co...  47.9 us
    dot_general x12, matrix products, spectral(): jnp.matmul(left_imag, signed, precision=highest)  22.9 us
    dot_general x12, matrix products, spectral(): jnp.matmul(left_real, signed, precision=highest)  21.2 us
    dot_general x12, matrix products, spectral(): jnp.matmul(signed, imag_part, precision=highest)  20.8 us
    dot_general x12, matrix products, spectral(): jnp.matmul(cos_table, real_part, precision=highest)  20.7 us
    dot_general x12, matrix products, spectral(): jnp.matmul(signed, real_part, precision=highest)  20.2 us
  transfers between devices with their start and end apart: 5, of which 1 were waited for; matrix products, arithmetic and copies ran while one was open for 1% of the time, Pallas kernels for 0%

commit v1 on v0

--- a/solution.py
+++ b/solution.py
@@ -127,7 +127,7 @@
     flat_probe = grad_probe.reshape(2 * mode_count * probe_size, probe_size)
     share = flat_probe.shape[0] // lax.axis_size("tile")
     start_row = lax.axis_index("tile") * share
-    probe_total = lax.psum(flat_probe, ("group", "tile"))
+    probe_total = lax.psum(lax.psum(flat_probe, "group"), "tile")
     probe_shard = lax.dynamic_slice_in_dim(probe_total, start_row, share, 0)
     object_total = lax.psum(object_squares, ("group", "tile"))
     probe_squares = jnp.sum(probe_total * probe_total)

time: 653 us -> 1040 us (1.59)
  the two profiles are of different devices: /device:TPU:1 before, /device:TPU:8 now
where the time goes in v1:
time: 1040 us; the launch traced here: 1030 us
  waiting for transfers between devices  639 us (61%)
  matrix products  163 us (16%)
  blocking collectives  114 us (11%)
  local copies, waits for them, and re-layouts  50.5 us (5%)
  between operations  28.3 us (3%)
  other arithmetic  19.2 us (2%)
  starting transfers between devices  13.7 us (1%)
    psum x2, waiting for transfers between devices, shards(): probe_total = lax.psum(lax.psum(flat_probe, 'group'), 'tile')  615 us
    psum x1, blocking collectives, shards(): object_total = lax.psum(object_squares, ('group', 'tile'))  114 us
    dynamic_update_slice x3, local copies, waits for them, and re-layouts, shards(): lax.dynamic_update_slice(grad_obj, previous + update, (anchor, row_at, co...  43 us
    ppermute x2, waiting for transfers between devices, passed_along(): return lax.ppermute(block, axis, route)  23.9 us
    dot_general x12, matrix products, spectral(): jnp.matmul(left_real, signed, precision=highest)  21.2 us
    dot_general x12, matrix products, spectral(): jnp.matmul(left_imag, signed, precision=highest)  21.1 us
  transfers between devices with their start and end apart: 6, of which 4 were waited for; matrix products, arithmetic and copies ran while one was open for 6% of the time, Pallas kernels for 0%

profile of v1, /device:TPU:8, one launch (start us, length us, event | category | flops | bytes accessed | tf_op | source)
XLA Modules:
  0.0 1027.6 jit_solution(12931380604742030447)
XLA Ops:
  7.2 3.6 collective-permute-start
  10.8 3.2 collective-permute-start.1
  42.6 2.0 fusion.156
  79.4 2.1 fusion.13
  86.2 2.4 add_reduce_fusion.3
  92.0 1.9 fusion.11
  116.8 2.1 add_reduce_fusion.6
  147.1 2.5 add_reduce_fusion
  154.7 2.0 fusion.110
  194.7 3.3 add_bitcast_fusion
  200.5 14.7 %dynamic_update_slice.9 = f32[4,512,384]{2,1,0:T(8,128)S(1)} dynamic-update-slice(f32[4,512,384]{2,1,0:T(8,128)S(1)} %broadcast_in_dim.2, f32[4,256,256]{2,1,0:T(8,128)} %pad_maximum_fusion, s32[]{:T(128)} %constant.21.clone.1, s32[]{:T(128)S(6)} %select_n.264, s32[]{:T(128)S(6)} %select_n.265) | dynamic-update-slice | bytes 2097156 | tf_op jit(solution)/shard_map/dynamic_update_slice | solution.py:120
  215.2 2.5 maximum_add_fusion
  217.6 14.2 %dynamic_update_slice.10 = f32[4,512,384]{2,1,0:T(8,128)S(1)} dynamic-update-slice(f32[4,512,384]{2,1,0:T(8,128)S(1)} %dynamic_update_slice.9, f32[4,256,256]{2,1,0:T(8,128)} %maximum_add_fusion, s32[]{:T(128)} %constant.21.clone.1, s32[]{:T(128)S(6)} %select_n.267, s32[]{:T(128)S(6)} %select_n.268) | dynamic-update-slice | bytes 2097156 | tf_op jit(solution)/shard_map/dynamic_update_slice | solution.py:120
  231.8 2.5 maximum_add_fusion.1
  234.4 14.2 %dynamic_update_slice.11 = f32[4,512,384]{2,1,0:T(8,128)S(1)} dynamic-update-slice(f32[4,512,384]{2,1,0:T(8,128)S(1)} %dynamic_update_slice.10, f32[4,256,256]{2,1,0:T(8,128)} %maximum_add_fusion.1, s32[]{:T(128)} %constant.21.clone.1, s32[]{:T(128)S(6)} %select_n.269, s32[]{:T(128)S(6)} %select_n.270) | dynamic-update-slice | bytes 2097156 | tf_op jit(solution)/shard_map/dynamic_update_slice | solution.py:120
  250.0 3.9 collective-permute-start.2
  253.9 2.9 collective-permute-start.3
  257.7 19.2 %collective-permute-done.2 = f32[4,512,128]{2,1,0:T(8,128)} collective-permute-done((f32[4,512,128]{2,1,0:T(8,128)}, f32[4,512,128]{2,1,0:T(8,128)}, u32[]{:S(2)}, u32[]{:S(2)}) %collective-permute-start.2) | collective-permute-done | bytes 1048608 | tf_op jit(solution)/shard_map/ppermute | solution.py:33
  276.9 4.6 collective-permute-done.3
  281.6 2.4 multiply_reduce_fusion.1
  284.0 114.2 %psum.21 = f32[]{:T(128)} all-reduce(f32[]{:T(128)} %multiply_reduce_fusion.1), channel_id=1, replica_groups=mesh['group'=4,'tile'=64] {'group','tile'}, use_global_device_ids=true, to_apply=%region_16.17 | all-reduce | flops 1 | bytes 8 | tf_op jit(solution)/shard_map/psum | solution.py:132
  398.9 3.0 slice_subtract_fusion
  402.0 614.2 %all-reduce.5.cloned.1.call-done = f32[1024,256]{1,0:T(8,128)} async-done(((f32[1024,256]{1,0:T(8,128)}), f32[1024,256]{1,0:T(8,128)}) %all-reduce.5.cloned.1.call-update) | async-done | bytes 1048592 | tf_op jit(solution)/shard_map/psum | solution.py:130
  1016.2 2.1 multiply_reduce_fusion
  (117 shorter events, 159.7 us)
Async XLA Ops:
  7.2 23.5 %copy-start.1 = (bf16[1,1,3,2,2,256,256]{6,5,4,3,2,1,0:T(8,128)(2,1)S(1)}, bf16[1,1,3,2,2,256,256]{6,5,4,3,2,1,0:T(8,128)(2,1)}, u32[]{:S(2)}) copy-start(bf16[1,1,3,2,2,256,256]{6,5,4,3,2,1,0:T(8,128)(2,1)} %param.8) | copy-start | bytes 4718596
  7.2 250.5 %all-reduce.3.cloned.1.call-start = ((), (), s32[]{:S(2)}) async-start(), calls=%async_computation | async-start | bytes 2097152 | tf_op jit(solution)/shard_map/psum | solution.py:130
  7.2 23.8 %collective-permute-start = (bf16[4,512,128]{2,1,0:T(8,128)(2,1)}, bf16[4,512,128]{2,1,0:T(8,128)(2,1)}, u32[]{:S(2)}, u32[]{:S(2)}) collective-permute-start(bf16[4,512,128]{2,1,0:T(8,128)(2,1)} %param.6), channel_id=1, source_target_pairs={{0,1},{1,2},{2,3},{3,4},{4,5},{5,6},{6,7},{7,8},{8,9},{9,10},{10,1... | collective-permute-start | bytes 1572872 | tf_op jit(solution)/shard_map/ppermute | solution.py:21
  10.8 20.1 %collective-permute-start.1 = (bf16[4,512,128]{2,1,0:T(8,128)(2,1)}, bf16[4,512,128]{2,1,0:T(8,128)(2,1)}, u32[]{:S(2)}, u32[]{:S(2)}) collective-permute-start(bf16[4,512,128]{2,1,0:T(8,128)(2,1)} %param.6), channel_id=1, source_target_pairs={{1,0},{2,1},{3,2},{4,3},{5,4},{6,5},{7,6},{8,7},{9,8},{10,9},{11,1... | collective-permute-start | bytes 1572872 | tf_op jit(solution)/shard_map/ppermute | solution.py:23
  25.8 5.2 copy-start.2
  32.4 1.7 copy-start
  69.4 4.8 copy-start.3
  199.2 817.0 %all-reduce.5.cloned.1.call-start = ((), (), s32[]{:S(2)}) async-start(), calls=%async_computation.1 | async-start | bytes 2097152 | tf_op jit(solution)/shard_map/psum | solution.py:130
  250.0 26.9 %collective-permute-start.2 = (f32[4,512,128]{2,1,0:T(8,128)}, f32[4,512,128]{2,1,0:T(8,128)}, u32[]{:S(2)}, u32[]{:S(2)}) collective-permute-start(f32[4,512,128]{2,1,0:T(8,128)} %get-tuple-element.30), channel_id=1, source_target_pairs={{1,0},{2,1},{3,2},{4,3},{5,4},{6,5},{7,6},{8,7},{9,8},{10,9},{11,1... | collective-permute-start | bytes 3145736 | tf_op jit(solution)/shard_map/ppermute | solution.py:33
  253.9 27.7 %collective-permute-start.3 = (f32[4,512,128]{2,1,0:T(8,128)}, f32[4,512,128]{2,1,0:T(8,128)}, u32[]{:S(2)}, u32[]{:S(2)}) collective-permute-start(f32[4,512,128]{2,1,0:T(8,128)} %get-tuple-element.31), channel_id=1, source_target_pairs={{0,1},{1,2},{2,3},{3,4},{4,5},{5,6},{6,7},{7,8},{8,9},{9,10},{10,1... | collective-permute-start | bytes 3145736 | tf_op jit(solution)/shard_map/ppermute | solution.py:33
Sparse Core Ops, SparseCore 0:
  199.3 58.2 all-reduce.2
  260.5 755.6 all-reduce.4
